TPU v7x, 32 devices: a whole 2x2x4 slice. The times are simulated.
32 devices in a mesh: groups: 2 (over x), seq: 16 (over z, y, core).
Axes of the slice: x: 2, y: 2, z: 4, core: 2. Of those that a mesh axis runs over, the one named last changes fastest.
Arguments:
- query: bfloat16 [8192, 1536], P(('groups', 'seq')), parts along dimension 0, may hold values from -6 to 6
- keys: bfloat16 [8192, 1536], P(('groups', 'seq')), parts along dimension 0, may hold values from -6 to 6
- values: bfloat16 [8192, 1536], P(('groups', 'seq')), parts along dimension 0, may hold values from -6 to 6
- allowed: int32 [64, 4], P(('groups', 'seq')), parts along dimension 0, may hold values from -1 to 31, as said below
- kernel: float32 [31, 1536], replicated, may hold values from -4 to 4
- cotangent: bfloat16 [8192, 1536], P(('groups', 'seq')), parts along dimension 0, may hold values from -6 to 6
Outputs:
- conv_out: bfloat16 [8192, 1536], P(('groups', 'seq')), parts along dimension 0
- query_grad: bfloat16 [8192, 1536], P(('groups', 'seq')), parts along dimension 0
- keys_grad: bfloat16 [8192, 1536], P(('groups', 'seq')), parts along dimension 0
- values_grad: bfloat16 [8192, 1536], P(('groups', 'seq')), parts along dimension 0
- kernel_grad: float32 [62, 1536], P('groups'), parts along dimension 0
There are 2 independent parts, one for each index of `groups`. A program takes and returns all parts, laid end to end along the dimension named above; an argument that names none is the same for every part. Nothing has to cross between parts.
Inputs may be any that keep to these rules, and one draw needn't show every extreme that they name: `allowed`: row b lists b first, then three distinct earlier blocks between b - 8 and b - 1, or -1 where such a block would lie before frame 0; the last row reaches back exactly 8 blocks.
All inputs are finite; a program needn't handle non-finite values.
Results may differ from a plain program's by a relative error of at most 0.012.
Values may be sent and summed in bfloat16 or wider, within the bound.
A program may use at most 128 MiB of HBM per device.

v0:
```python
import jax
import jax.numpy as jnp
from jax import lax
from jax.sharding import PartitionSpec as P

HD = 64
KERNEL = 31
BLOCK = 128
SPAN_DEV = 4
SCALE = 0.125
NEG = -1e30


def shifted(block, axis, distance):
    devices = range(lax.axis_size(axis))
    route = [(i - distance, i) for i in devices if i - distance in devices]
    return lax.ppermute(block, axis, route)


def with_halo(block, sides, width):
    for axis, dim in sides:
        count = lax.axis_size(axis)
        forward = [(i, i + 1) for i in range(count - 1)]
        backward = [(target, source) for source, target in forward]
        low = lax.ppermute(
            lax.slice_in_dim(block, block.shape[dim] - width, None, axis=dim), axis, forward
        )
        high = lax.ppermute(lax.slice_in_dim(block, 0, width, axis=dim), axis, backward)
        block = jnp.concatenate([low, block, high], axis=dim)
    return block


def head_major(matrix, heads):
    return matrix.reshape(matrix.shape[0], heads, HD).transpose(1, 0, 2)


def row_major(array):
    return array.transpose(1, 0, 2).reshape(array.shape[1], array.shape[0] * array.shape[2])


def attend(query_head, key_head, frame_ok):
    scores = jnp.dot(query_head, key_head.T, preferred_element_type=jnp.float32) * SCALE
    scores = jnp.where(frame_ok, scores, NEG)
    peak = jnp.max(scores, axis=-1, keepdims=True)
    expo = jnp.exp(scores - peak)
    total = jnp.sum(expo, axis=-1, keepdims=True)
    return (expo / total, peak[:, 0] + jnp.log(total[:, 0]))


def local(query, keys, values, allowed, kernel, cotangent):
    frames, width = query.shape
    heads = width // HD
    blocks_dev = frames // BLOCK
    half = KERNEL // 2
    own_index = lax.axis_index("seq")
    stacked = jnp.stack([keys, values])
    pieces = [stacked]
    carried = stacked
    for distance in range(1, SPAN_DEV + 1):
        carried = shifted(carried, "seq", 1)
        pieces.append(carried)
    candidates = jnp.concatenate(pieces, axis=1)
    key_ids = jnp.concatenate(
        [
            own_index * blocks_dev - distance * blocks_dev + jnp.arange(blocks_dev, dtype=jnp.int32)
            for distance in range(SPAN_DEV + 1)
        ]
    )
    block_ok = (
        jnp.any(allowed[:, :, None] == key_ids[None, None, :], axis=1) & (key_ids >= 0)[None, :]
    )
    frame_ok = jnp.repeat(jnp.repeat(block_ok, BLOCK, axis=0), BLOCK, axis=1)
    query_heads = head_major(query, heads)
    key_heads = head_major(candidates[0], heads)
    value_heads = head_major(candidates[1], heads)

    def forward_head(inputs):
        query_head, key_head, value_head = inputs
        probs, log_total = attend(query_head, key_head, frame_ok)
        return (
            jnp.dot(probs.astype(jnp.bfloat16), value_head, preferred_element_type=jnp.float32),
            log_total,
        )

    attended_heads, log_totals = lax.map(forward_head, (query_heads, key_heads, value_heads))
    attended = row_major(attended_heads)
    attended_half = attended.astype(jnp.bfloat16)
    padded = with_halo(attended_half, (("seq", 0),), KERNEL // 2)
    cot_pad = with_halo(cotangent, (("seq", 0),), KERNEL // 2)
    cot_float = cotangent.astype(jnp.float32)
    conv_sum = jnp.zeros((frames, width), jnp.float32)
    grad_sum = jnp.zeros((frames, width), jnp.float32)
    taps_grad = []
    for offset in range(KERNEL):
        window = padded[offset : offset + frames].astype(jnp.float32)
        conv_sum = conv_sum + kernel[offset][None, :] * window
        grad_sum = grad_sum + kernel[offset][None, :] * cot_pad[
            2 * half - offset : 2 * half - offset + frames
        ].astype(jnp.float32)
        taps_grad.append(jnp.sum(cot_float * window, axis=0))
    conv_out = conv_sum.astype(jnp.bfloat16)
    attended_grad = grad_sum.astype(jnp.bfloat16)
    kernel_grad = lax.psum(jnp.stack(taps_grad), "seq")
    grad_heads = head_major(attended_grad, heads)
    out_heads = head_major(attended, heads)
    deltas = jnp.sum(grad_heads.astype(jnp.float32) * out_heads, axis=-1)

    def backward_head(inputs):
        query_head, key_head, value_head, grad_head, delta_head = inputs
        probs, unused = attend(query_head, key_head, frame_ok)
        probs_half = probs.astype(jnp.bfloat16)
        probs_grad = jnp.dot(grad_head, value_head.T, preferred_element_type=jnp.float32)
        scores_grad = (SCALE * probs * (probs_grad - delta_head[:, None])).astype(jnp.bfloat16)
        query_part = jnp.dot(scores_grad, key_head, preferred_element_type=jnp.float32)
        keys_part = jnp.einsum(
            "qk,qd->kd", scores_grad, query_head, preferred_element_type=jnp.float32
        )
        values_part = jnp.einsum(
            "qk,qd->kd", probs_half, grad_head, preferred_element_type=jnp.float32
        )
        return (query_part, keys_part, values_part)

    query_part, keys_part, values_part = lax.map(
        backward_head, (query_heads, key_heads, value_heads, grad_heads, deltas)
    )
    query_grad = row_major(query_part).astype(jnp.bfloat16)
    grads = jnp.stack([row_major(keys_part), row_major(values_part)])
    terms = [
        grads[:, distance * frames : (distance + 1) * frames] for distance in range(SPAN_DEV + 1)
    ]
    totals = terms[SPAN_DEV]
    for distance in range(SPAN_DEV - 1, -1, -1):
        totals = (
            shifted(totals.astype(jnp.bfloat16), "seq", -1).astype(totals.dtype) + terms[distance]
        )
    keys_total = totals[0]
    values_total = totals[1]
    keys_grad = keys_total.astype(jnp.bfloat16)
    values_grad = values_total.astype(jnp.bfloat16)
    return (conv_out, query_grad, keys_grad, values_grad, kernel_grad)


def solution(mesh):
    placed = (
        P(("groups", "seq"), None),
        P(("groups", "seq"), None),
        P(("groups", "seq"), None),
        P(("groups", "seq"), None),
        P(),
        P(("groups", "seq"), None),
    )
    return jax.shard_map(
        local,
        mesh=mesh,
        in_specs=placed,
        out_specs=(
            P(("groups", "seq"), None),
            P(("groups", "seq"), None),
            P(("groups", "seq"), None),
            P(("groups", "seq"), None),
            P("groups", None),
        ),
        check_vma=False,
    )
```

profile of v0, /device:TPU:0, one launch (start us, length us, event | category | flops | bytes accessed | tf_op | source)
XLA Modules:
  0.0 679.3 jit_solution(14867233980165950894)
XLA Ops:
  10.4 2.4 collective-permute-start
  12.9 2.9 collective-permute-done
  17.0 20.1 %collective-permute-start.1 = (bf16[2,256,1536]{1,2,0:T(8,128)(2,1)S(1)}, bf16[2,256,1536]{1,2,0:T(8,128)(2,1)}, u32[]{:S(2)}, u32[]{:S(2)}) collective-permute-start(bf16[2,256,1536]{1,2,0:T(8,128)(2,1)S(1)} %collective-permute-done), channel_id=1, source_target_pairs={{0,1},{1,2},{2,3},{3,4},{4,5},{5,6},{6,7},{7,8},{8,9},{9,10},{10,1... | collective-permute-start | bytes 4718600 | tf_op jit(solution)/shard_map/ppermute | solution.py:17
  39.0 19.7 %collective-permute-start.2 = (bf16[2,256,1536]{1,2,0:T(8,128)(2,1)}, bf16[2,256,1536]{1,2,0:T(8,128)(2,1)}, u32[]{:S(2)}, u32[]{:S(2)}) collective-permute-start(bf16[2,256,1536]{1,2,0:T(8,128)(2,1)} %collective-permute-done.1), channel_id=1, source_target_pairs={{0,1},{1,2},{2,3},{3,4},{4,5},{5,6},{6,7},{7,8},{8,9},{9,10},{10,1... | collective-permute-start | bytes 4718600 | tf_op jit(solution)/shard_map/ppermute | solution.py:17
  59.7 3.4 collective-permute-start.7
  65.7 2.1 slice_reduce_fusion.29
  67.8 2.5 slice_reduce_fusion.30
  72.8 11.2 %collective-permute-start.3 = (bf16[2,256,1536]{1,2,0:T(8,128)(2,1)}, bf16[2,256,1536]{1,2,0:T(8,128)(2,1)S(1)}, u32[]{:S(2)}, u32[]{:S(2)}) collective-permute-start(bf16[2,256,1536]{1,2,0:T(8,128)(2,1)} %collective-permute-done.2), channel_id=1, source_target_pairs={{0,1},{1,2},{2,3},{3,4},{4,5},{5,6},{6,7},{7,8},{8,9},{9,10},{10,1... | collective-permute-start | bytes 4718600 | tf_op jit(solution)/shard_map/ppermute | solution.py:17
  84.0 27.4 %fusion.136 = bf16[256,1536]{0,1:T(8,128)(2,1)} fusion(bf16[256,1536]{0,1:T(8,128)(2,1)S(1)} %copy.71, bf16[15,1536]{0,1:T(8,128)(2,1)S(1)} %collective-permute-done.7, bf16[15,1536]{0,1:T(8,128)(2,1)} %collective-permute-done.6, f32[1536]{0:T(1024)} %get-tuple-element.256, f32[1536]{0:T(1024)} %get-tuple-element.257, f32[1536]{0:T(1024)} %get-tuple-element.228, ...), kind=kLoop, calls=%fused_computation.330 | loop fusion | flops 71958528 | bytes 1855488 | tf_op jit(solution)/shard_map/convert_element_type | solution.py:102
  112.8 2.7 constant_dynamic-update-slice_fusion.2
  115.5 2.8 constant_dynamic-update-slice_fusion.1
  119.7 5.6 fusion.195
  125.2 8.3 %copy.68 = bf16[24,1280,64]{2,1,0:T(8,128)(2,1)} copy(bf16[24,1280,64]{1,2,0:T(8,128)(2,1)} %bitcast.179) | data formatting | bytes 7864320
  133.5 8.2 %copy.69 = bf16[24,1280,64]{2,1,0:T(8,128)(2,1)} copy(bf16[24,1280,64]{1,2,0:T(8,128)(2,1)} %bitcast.178) | data formatting | bytes 7864320
  141.7 104.6 %while.28 = (s32[]{:T(128)}, f32[24,256,64]{1,2,0:T(8,128)}, bf16[24,256,64]{2,1,0:T(8,128)(2,1)S(1)}, bf16[24,1280,64]{2,1,0:T(8,128)(2,1)}, bf16[24,1280,64]{2,1,0:T(8,128)(2,1)}, /*index=5*/pred[256,10]{0,1:T(8,128)(4,1)S(1)}) while((s32[]{:T(128)}, f32[24,256,64]{1,2,0:T(8,128)}, ...), condition=%wide.region_4.5_spmd.clone.clone, body=%wide.region_1.4_spmd.clone.sunk.clone | while | flops 86507008 | bytes 6039117 | solution.py:85
  152.7 2.1 fusion.239
  157.1 2.1 fusion.239
  170.1 2.1 fusion.239
  174.5 2.1 fusion.239
  178.9 2.1 fusion.239
  183.2 2.1 fusion.239
  187.6 2.1 fusion.239
  191.9 2.1 fusion.239
  196.3 2.1 fusion.239
  200.7 2.1 fusion.239
  205.0 2.1 fusion.239
  213.7 2.1 fusion.239
  222.4 2.1 fusion.239
  226.8 2.1 fusion.239
  231.2 2.1 fusion.239
  239.9 2.1 fusion.239
  244.2 2.1 fusion.239
  246.3 2.5 multiply_reduce_fusion
  248.8 208.7 %while.29 = (s32[]{:T(128)}, bf16[24,256,64]{1,2,0:T(8,128)(2,1)}, f32[24,1280,64]{1,2,0:T(8,128)}, f32[24,1280,64]{1,2,0:T(8,128)}, bf16[24,256,64]{2,1,0:T(8,1...) while((s32[]{:T(128)}, bf16[24,256,64]{1,2,0:T(8,128)(2,1)}, ...), condition=%wide.region_9.10_spmd.clone.clone, body=%wide.region_6.9_spmd.clone.sunk.clone | while | flops 214302208 | bytes 10438257 | solution.py:123
  457.5 2.3 fusion.49
  461.4 6.0 collective-permute-done.8
  471.4 20.0 %collective-permute-start.4 = (bf16[15,1536]{0,1:T(8,128)(2,1)}, bf16[15,1536]{0,1:T(8,128)(2,1)S(1)}, u32[]{:S(2)}, u32[]{:S(2)}) collective-permute-start(bf16[15,1536]{0,1:T(8,128)(2,1)} %bitcast.9), channel_id=1, source_target_pairs={{0,1},{1,2},{2,3},{3,4},{4,5},{5,6},{6,7},{7,8},{8,9},{9,10},{10,1... | collective-permute-start | bytes 138248 | tf_op jit(solution)/shard_map/ppermute | solution.py:25
  494.0 5.7 fusion.119
  500.0 2.9 fusion.55
  504.6 19.3 %fusion.88 = bf16[256,1536]{0,1:T(8,128)(2,1)S(1)} fusion(bf16[256,1536]{0,1:T(8,128)(2,1)S(1)} %bitcast.172, f32[1536]{0:T(1024)S(1)} %copy-done.35, f32[1536]{0:T(1024)S(1)} %copy-done.36, f32[1536]{0:T(1024)S(1)} %copy-done.7, f32[1536]{0:T(1024)S(1)} %copy-done.8, f32[1536]{0:T(1024)S(1)} %copy-done.9, f32[1536]{0:T(1024)S(1)} %copy-done.10, ...), kind=kLoop, calls=%fused_computation.280 | loop fusion | flops 71958528 | bytes 1855488 | tf_op jit(solution)/shard_map/convert_element_type | solution.py:101
  523.9 4.6 collective-permute-done.10
  531.4 3.7 fusion.118
  536.4 6.0 fusion.135
  542.4 4.4 fusion.134
  547.0 2.8 stack.143
  549.8 3.0 collective-permute-done.11
  552.8 2.7 fusion.57
  557.9 112.9 %all-reduce.2.cloned.1.call-done = f32[31,1536]{1,0:T(8,128)} async-done(((f32[31,1536]{1,0:T(8,128)}), f32[31,1536]{1,0:T(8,128)}) %all-reduce.2.cloned.1.call-update) | async-done | bytes 190480 | tf_op jit(solution)/shard_map/psum | solution.py:103
  (492 shorter events, 310.2 us)
Async XLA Ops:
  7.2 663.7 %all-reduce.2.cloned.1.call-start = ((), (), s32[]{:S(2)}) async-start(), calls=%async_computation | async-start | bytes 393216 | tf_op jit(solution)/shard_map/psum | solution.py:103
  9.0 49.7 %copy-start.4 = (bf16[256,1536]{1,0:T(8,128)(2,1)S(1)}, bf16[256,1536]{1,0:T(8,128)(2,1)}, u32[]{:S(2)}) copy-start(bf16[256,1536]{1,0:T(8,128)(2,1)} %param.15) | copy-start | bytes 2359300
  9.0 56.5 %copy-start.37 = (s32[2,4]{1,0:T(2,128)S(1)}, s32[2,4]{1,0:T(2,128)}, u32[]{:S(2)}) copy-start(s32[2,4]{1,0:T(2,128)} %param.13) | copy-start | bytes 100
  10.4 5.4 collective-permute-start
  17.0 22.0 %collective-permute-start.1 = (bf16[2,256,1536]{1,2,0:T(8,128)(2,1)S(1)}, bf16[2,256,1536]{1,2,0:T(8,128)(2,1)}, u32[]{:S(2)}, u32[]{:S(2)}) collective-permute-start(bf16[2,256,1536]{1,2,0:T(8,128)(2,1)S(1)} %collective-permute-done), channel_id=1, source_target_pairs={{0,1},{1,2},{2,3},{3,4},{4,5},{5,6},{6,7},{7,8},{8,9},{9,10},{10,1... | collective-permute-start | bytes 4718600 | tf_op jit(solution)/shard_map/ppermute | solution.py:17
  39.0 33.9 %collective-permute-start.2 = (bf16[2,256,1536]{1,2,0:T(8,128)(2,1)}, bf16[2,256,1536]{1,2,0:T(8,128)(2,1)}, u32[]{:S(2)}, u32[]{:S(2)}) collective-permute-start(bf16[2,256,1536]{1,2,0:T(8,128)(2,1)} %collective-permute-done.1), channel_id=1, source_target_pairs={{0,1},{1,2},{2,3},{3,4},{4,5},{5,6},{6,7},{7,8},{8,9},{9,10},{10,1... | collective-permute-start | bytes 4718600 | tf_op jit(solution)/shard_map/ppermute | solution.py:17
  59.7 24.3 %collective-permute-start.7 = (bf16[15,1536]{0,1:T(8,128)(2,1)}, bf16[15,1536]{0,1:T(8,128)(2,1)S(1)}, u32[]{:S(2)}, u32[]{:S(2)}) collective-permute-start(bf16[15,1536]{0,1:T(8,128)(2,1)} %copy.73), channel_id=1, source_target_pairs={{0,1},{1,2},{2,3},{3,4},{4,5},{5,6},{6,7},{7,8},{8,9},{9,10},{10,1... | collective-permute-start | bytes 138248 | tf_op jit(solution)/shard_map/ppermute | solution.py:25
  63.1 8.6 %copy-start.6 = (bf16[256,1536]{1,0:T(8,128)(2,1)S(1)}, bf16[256,1536]{1,0:T(8,128)(2,1)}, u32[]{:S(2)}) copy-start(bf16[256,1536]{1,0:T(8,128)(2,1)} %param.10) | copy-start | bytes 2359300
  64.0 20.0 %collective-permute-start.6 = (bf16[15,1536]{0,1:T(8,128)(2,1)}, bf16[15,1536]{0,1:T(8,128)(2,1)}, u32[]{:S(2)}, u32[]{:S(2)}) collective-permute-start(bf16[15,1536]{0,1:T(8,128)(2,1)} %copy.70), channel_id=1, source_target_pairs={{1,0},{2,1},{3,2},{4,3},{5,4},{6,5},{7,6},{8,7},{9,8},{10,9},{11,1... | collective-permute-start | bytes 138248 | tf_op jit(solution)/shard_map/ppermute | solution.py:28
  72.8 38.6 %copy-start.3 = (bf16[2,256,1536]{1,2,0:T(8,128)(2,1)S(1)}, bf16[2,256,1536]{1,2,0:T(8,128)(2,1)}, u32[]{:S(2)}) copy-start(bf16[2,256,1536]{1,2,0:T(8,128)(2,1)} %copy-done.2) | copy-start | bytes 4718596
  72.8 45.5 %collective-permute-start.3 = (bf16[2,256,1536]{1,2,0:T(8,128)(2,1)}, bf16[2,256,1536]{1,2,0:T(8,128)(2,1)S(1)}, u32[]{:S(2)}, u32[]{:S(2)}) collective-permute-start(bf16[2,256,1536]{1,2,0:T(8,128)(2,1)} %collective-permute-done.2), channel_id=1, source_target_pairs={{0,1},{1,2},{2,3},{3,4},{4,5},{5,6},{6,7},{7,8},{8,9},{9,10},{10,1... | collective-permute-start | bytes 4718600 | tf_op jit(solution)/shard_map/ppermute | solution.py:17
  457.5 9.9 %slice-start = ((s8[7864320]{0:T(1024)(128)(4,1)}), s8[4194304]{0:T(1024)(128)(4,1)S(1)}, s32[]{:S(2)}) async-start(s8[7864320]{0:T(1024)(128)(4,1)} %bitcast.157), calls=%async_computation.1 | async-start | bytes 8388608
  457.5 9.9 %slice-start.1 = ((s8[7864320]{0:T(1024)(128)(4,1)}), s8[3670016]{0:T(1024)(128)(4,1)S(1)}, s32[]{:S(2)}) async-start(s8[7864320]{0:T(1024)(128)(4,1)} %bitcast.157), calls=%async_computation.2 | async-start | bytes 7340032
  457.5 9.9 %copy-start = (f32[24,1280,64]{1,2,0:T(8,128)S(1)}, f32[24,1280,64]{1,2,0:T(8,128)}, u32[]{:S(2)}) copy-start(f32[24,1280,64]{1,2,0:T(8,128)} %get-tuple-element.93) | copy-start | bytes 23592964
  459.8 7.6 %collective-permute-start.8 = (bf16[2,256,1536]{1,2,0:T(8,128)(2,1)S(1)}, bf16[2,256,1536]{1,2,0:T(8,128)(2,1)S(1)}, u32[]{:S(2)}, u32[]{:S(2)}) collective-permute-start(bf16[2,256,1536]{1,2,0:T(8,128)(2,1)S(1)} %fusion.49), channel_id=1, source_target_pairs={{1,0},{2,1},{3,2},{4,3},{5,4},{6,5},{7,6},{8,7},{9,8},{10,9},{11,1... | collective-permute-start | bytes 4718600 | tf_op jit(solution)/shard_map/ppermute | solution.py:17
  469.1 22.4 %copy-start.1 = (bf16[24,256,64]{1,2,0:T(8,128)(2,1)S(1)}, bf16[24,256,64]{1,2,0:T(8,128)(2,1)}, u32[]{:S(2)}) copy-start(bf16[24,256,64]{1,2,0:T(8,128)(2,1)} %get-tuple-element.92) | copy-start | bytes 2359300
  469.1 30.9 %collective-permute-start.9 = (bf16[2,256,1536]{1,2,0:T(8,128)(2,1)}, bf16[2,256,1536]{1,2,0:T(8,128)(2,1)}, u32[]{:S(2)}, u32[]{:S(2)}) collective-permute-start(bf16[2,256,1536]{1,2,0:T(8,128)(2,1)} %fusion.52), channel_id=1, source_target_pairs={{1,0},{2,1},{3,2},{4,3},{5,4},{6,5},{7,6},{8,7},{9,8},{10,9},{11,1... | collective-permute-start | bytes 4718600 | tf_op jit(solution)/shard_map/ppermute | solution.py:17
  471.4 22.5 %collective-permute-start.4 = (bf16[15,1536]{0,1:T(8,128)(2,1)}, bf16[15,1536]{0,1:T(8,128)(2,1)S(1)}, u32[]{:S(2)}, u32[]{:S(2)}) collective-permute-start(bf16[15,1536]{0,1:T(8,128)(2,1)} %bitcast.9), channel_id=1, source_target_pairs={{0,1},{1,2},{2,3},{3,4},{4,5},{5,6},{6,7},{7,8},{8,9},{9,10},{10,1... | collective-permute-start | bytes 138248 | tf_op jit(solution)/shard_map/ppermute | solution.py:25
  492.6 11.7 %collective-permute-start.5 = (bf16[15,1536]{0,1:T(8,128)(2,1)S(1)}, bf16[15,1536]{0,1:T(8,128)(2,1)S(1)}, u32[]{:S(2)}, u32[]{:S(2)}) collective-permute-start(bf16[15,1536]{0,1:T(8,128)(2,1)S(1)} %bitcast.187), channel_id=1, source_target_pairs={{1,0},{2,1},{3,2},{4,3},{5,4},{6,5},{7,6},{8,7},{9,8},{10,9},{11,1... | collective-permute-start | bytes 138248 | tf_op jit(solution)/shard_map/ppermute | solution.py:28
  493.9 34.5 %slice-start.2 = ((s8[7864320]{0:T(1024)(128)(4,1)}), s8[4194304]{0:T(1024)(128)(4,1)S(1)}, s32[]{:S(2)}) async-start(s8[7864320]{0:T(1024)(128)(4,1)} %bitcast.160), calls=%async_computation.3 | async-start | bytes 8388608
  493.9 34.5 %slice-start.4 = ((s8[7864320]{0:T(1024)(128)(4,1)}), s8[4194304]{0:T(1024)(128)(4,1)S(1)}, s32[]{:S(2)}) async-start(s8[7864320]{0:T(1024)(128)(4,1)} %bitcast.167), calls=%async_computation.5 | async-start | bytes 8388608
  499.6 4.7 copy-start.7
  499.6 4.7 copy-start.8
  499.6 4.7 copy-start.9
  499.7 4.7 copy-start.10
  499.7 4.7 copy-start.11
  499.7 4.7 copy-start.12
  499.7 4.7 copy-start.13
  499.7 4.7 copy-start.14
  499.7 4.7 copy-start.15
  499.7 4.7 copy-start.16
  499.7 4.7 copy-start.17
  499.7 4.7 copy-start.18
  499.7 4.7 copy-start.19
  499.8 4.7 copy-start.20
  499.8 4.7 copy-start.21
  499.8 4.7 copy-start.22
  499.8 4.7 copy-start.23
  499.8 4.7 copy-start.24
  499.8 4.7 copy-start.25
  499.8 4.7 copy-start.26
  499.8 4.7 copy-start.27
  499.8 4.7 copy-start.28
  499.8 4.7 copy-start.29
  499.9 28.5 %slice-start.3 = ((s8[7864320]{0:T(1024)(128)(4,1)}), s8[3670016]{0:T(1024)(128)(4,1)S(1)}, s32[]{:S(2)}) async-start(s8[7864320]{0:T(1024)(128)(4,1)} %bitcast.160), calls=%async_computation.4 | async-start | bytes 7340032
  499.9 28.5 %slice-start.5 = ((s8[7864320]{0:T(1024)(128)(4,1)}), s8[3670016]{0:T(1024)(128)(4,1)S(1)}, s32[]{:S(2)}) async-start(s8[7864320]{0:T(1024)(128)(4,1)} %bitcast.167), calls=%async_computation.6 | async-start | bytes 7340032
  502.9 25.6 %collective-permute-start.10 = (bf16[2,256,1536]{1,2,0:T(8,128)(2,1)S(1)}, bf16[2,256,1536]{1,2,0:T(8,128)(2,1)S(1)}, u32[]{:S(2)}, u32[]{:S(2)}) collective-permute-start(bf16[2,256,1536]{1,2,0:T(8,128)(2,1)S(1)} %fusion.55), channel_id=1, source_target_pairs={{1,0},{2,1},{3,2},{4,3},{5,4},{6,5},{7,6},{8,7},{9,8},{10,9},{11,1... | collective-permute-start | bytes 4718600 | tf_op jit(solution)/shard_map/ppermute | solution.py:17
  530.1 22.7 %collective-permute-start.11 = (bf16[2,256,1536]{1,2,0:T(8,128)(2,1)}, bf16[2,256,1536]{1,2,0:T(8,128)(2,1)}, u32[]{:S(2)}, u32[]{:S(2)}) collective-permute-start(bf16[2,256,1536]{1,2,0:T(8,128)(2,1)} %fusion.47), channel_id=1, source_target_pairs={{1,0},{2,1},{3,2},{4,3},{5,4},{6,5},{7,6},{8,7},{9,8},{10,9},{11,1... | collective-permute-start | bytes 4718600 | tf_op jit(solution)/shard_map/ppermute | solution.py:17
  (9 other events, 35.4 us)
Sparse Core Ops, SparseCore 0:
  549.9 120.8 all-reduce.1
where the time goes:
time: 686 us; the launch traced here: 679 us
  matrix products  272 us (40%)
  waiting for transfers between devices  131 us (19%)
  other arithmetic  99.1 us (14%)
  starting transfers between devices  85.1 us (12%)
  local copies, waits for them, and re-layouts  76.1 us (11%)
  between operations  15.2 us (2%)
    psum x1, waiting for transfers between devices, local(): kernel_grad = lax.psum(jnp.stack(taps_grad), 'seq')  113 us
    dot_general x48, matrix products, attend(): jnp.dot(query_head, key_head.T, preferred_element_type=jnp.float32) * SCALE  69 us
    ppermute x8, starting transfers between devices, shifted(): return lax.ppermute(block, axis, route)  59.1 us
    dot_general x24, matrix products, forward_head(): jnp.dot(probs.astype(jnp.bfloat16), value_head, preferred_element_type=jn...  49.4 us
    dot_general x24, matrix products, backward_head(): jnp.dot(scores_grad, key_head, preferred_element_type=jnp.float32)  46.7 us
    dot_general x24, matrix products, backward_head(): jnp.einsum('qk,qd->kd', probs_half, grad_head, preferred_element_type=jnp...  45.8 us
    dot_general x24, matrix products, backward_head(): jnp.dot(grad_head, value_head.T, preferred_element_type=jnp.float32)  36.4 us
    unnamed x106, local copies, waits for them, and re-layouts  34.1 us
  transfers between devices with their start and end apart: 13, of which 6 were waited for; matrix products, arithmetic and copies ran while one was open for 14% of the time, Pallas kernels for 0%

commit v1 on v0

--- a/solution.py
+++ b/solution.py
@@ -100,7 +100,7 @@
         taps_grad.append(jnp.sum(cot_float * window, axis=0))
     conv_out = conv_sum.astype(jnp.bfloat16)
     attended_grad = grad_sum.astype(jnp.bfloat16)
-    kernel_grad = lax.psum(jnp.stack(taps_grad), "seq")
+    kernel_grad = jnp.sum(lax.all_gather(jnp.stack(taps_grad), "seq"), axis=0)
     grad_heads = head_major(attended_grad, heads)
     out_heads = head_major(attended, heads)
     deltas = jnp.sum(grad_heads.astype(jnp.float32) * out_heads, axis=-1)

time: 686 us -> 624 us (0.910)
  the two profiles are of different devices: /device:TPU:0 before, /device:TPU:25 now
where the time goes in v1:
time: 624 us; the launch traced here: 617 us
  matrix products  272 us (44%)
  waiting for transfers between devices  115 us (18%)
  other arithmetic  105 us (17%)
  local copies, waits for them, and re-layouts  73.7 us (12%)
  starting transfers between devices  35.1 us (6%)
  between operations  15.1 us (2%)
    ppermute x8, waiting for transfers between devices, shifted(): return lax.ppermute(block, axis, route)  74.6 us
    dot_general x48, matrix products, attend(): jnp.dot(query_head, key_head.T, preferred_element_type=jnp.float32) * SCALE  69 us
    dot_general x24, matrix products, forward_head(): jnp.dot(probs.astype(jnp.bfloat16), value_head, preferred_element_type=jn...  49.4 us
    dot_general x24, matrix products, backward_head(): jnp.dot(scores_grad, key_head, preferred_element_type=jnp.float32)  46.7 us
    dot_general x24, matrix products, backward_head(): jnp.einsum('qk,qd->kd', probs_half, grad_head, preferred_element_type=jnp...  45.8 us
    ppermute x2, waiting for transfers between devices, with_halo(): lax.ppermute(lax.slice_in_dim(block, 0, width, axis=dim), axis, backward)  38.2 us
    dot_general x24, matrix products, backward_head(): jnp.dot(grad_head, value_head.T, preferred_element_type=jnp.float32)  36.4 us
    unnamed x95, local copies, waits for them, and re-layouts  32.5 us
  transfers between devices with their start and end apart: 13, of which 8 were waited for; matrix products, arithmetic and copies ran while one was open for 16% of the time, Pallas kernels for 0%

profile of v1, /device:TPU:25, one launch (start us, length us, event | category | flops | bytes accessed | tf_op | source)
XLA Modules:
  0.0 617.1 jit_solution(13016545467127315480)
XLA Ops:
  10.4 3.7 collective-permute-start
  14.2 17.3 %collective-permute-done = bf16[2,256,1536]{1,2,0:T(8,128)(2,1)S(1)} collective-permute-done((bf16[2,256,1536]{1,2,0:T(8,128)(2,1)S(1)}, bf16[2,256,1536]{1,2,0:T(8,128)(2,1)S(1)}, u32[]{:S(2)}, u32[]{:S(2)}) %collective-permute-start) | collective-permute-done | bytes 1572896 | tf_op jit(solution)/shard_map/ppermute | solution.py:17
  32.6 4.4 collective-permute-start.1
  37.0 17.3 %collective-permute-done.1 = bf16[2,256,1536]{1,2,0:T(8,128)(2,1)} collective-permute-done((bf16[2,256,1536]{1,2,0:T(8,128)(2,1)S(1)}, bf16[2,256,1536]{1,2,0:T(8,128)(2,1)}, u32[]{:S(2)}, u32[]{:S(2)}) %collective-permute-start.1) | collective-permute-done | bytes 1572896 | tf_op jit(solution)/shard_map/ppermute | solution.py:17
  54.4 4.5 collective-permute-start.2
  62.7 2.6 collective-permute-start.6
  65.7 2.1 slice_reduce_fusion.29
  67.8 2.5 slice_reduce_fusion.30
  72.8 3.7 collective-permute-done.2
  76.5 4.4 collective-permute-start.3
  80.9 24.2 %collective-permute-done.6 = bf16[15,1536]{0,1:T(8,128)(2,1)} collective-permute-done((bf16[15,1536]{0,1:T(8,128)(2,1)}, bf16[15,1536]{0,1:T(8,128)(2,1)}, u32[]{:S(2)}, u32[]{:S(2)}) %collective-permute-start.6) | collective-permute-done | bytes 46112 | tf_op jit(solution)/shard_map/ppermute | solution.py:28
  105.2 27.4 %fusion.136 = bf16[256,1536]{0,1:T(8,128)(2,1)} fusion(bf16[256,1536]{0,1:T(8,128)(2,1)S(1)} %copy.92, bf16[15,1536]{0,1:T(8,128)(2,1)S(1)} %collective-permute-done.7, bf16[15,1536]{0,1:T(8,128)(2,1)} %collective-permute-done.6, f32[1536]{0:T(1024)} %get-tuple-element.277, f32[1536]{0:T(1024)} %get-tuple-element.278, f32[1536]{0:T(1024)} %get-tuple-element.249, ...), kind=kLoop, calls=%fused_computation.330 | loop fusion | flops 71958528 | bytes 1855488 | tf_op jit(solution)/shard_map/convert_element_type | solution.py:102
  133.9 2.7 constant_dynamic-update-slice_fusion.2
  136.6 2.8 constant_dynamic-update-slice_fusion.1
  140.7 5.6 fusion.195
  146.3 8.3 %copy.89 = bf16[24,1280,64]{2,1,0:T(8,128)(2,1)} copy(bf16[24,1280,64]{1,2,0:T(8,128)(2,1)} %bitcast.174) | data formatting | bytes 7864320
  154.5 8.2 %copy.90 = bf16[24,1280,64]{2,1,0:T(8,128)(2,1)} copy(bf16[24,1280,64]{1,2,0:T(8,128)(2,1)} %bitcast.173) | data formatting | bytes 7864320
  162.8 104.6 %while.28 = (s32[]{:T(128)}, f32[24,256,64]{1,2,0:T(8,128)}, bf16[24,256,64]{2,1,0:T(8,128)(2,1)S(1)}, bf16[24,1280,64]{2,1,0:T(8,128)(2,1)}, bf16[24,1280,64]{2,1,0:T(8,128)(2,1)}, /*index=5*/pred[256,10]{0,1:T(8,128)(4,1)S(1)}) while((s32[]{:T(128)}, f32[24,256,64]{1,2,0:T(8,128)}, ...), condition=%wide.region_4.5_spmd.clone.clone, body=%wide.region_1.4_spmd.clone.sunk.clone | while | flops 86507008 | bytes 6039117 | solution.py:85
  178.1 2.1 fusion.239
  191.2 2.1 fusion.239
  204.3 2.1 fusion.239
  208.6 2.1 fusion.239
  217.4 2.1 fusion.239
  221.7 2.1 fusion.239
  243.5 2.1 fusion.239
  247.9 2.1 fusion.239
  252.2 2.1 fusion.239
  265.3 2.1 fusion.239
  267.4 2.5 multiply_reduce_fusion
  269.9 208.7 %while.29 = (s32[]{:T(128)}, bf16[24,256,64]{1,2,0:T(8,128)(2,1)}, f32[24,1280,64]{1,2,0:T(8,128)}, f32[24,1280,64]{1,2,0:T(8,128)}, bf16[24,256,64]{2,1,0:T(8,1...) while((s32[]{:T(128)}, bf16[24,256,64]{1,2,0:T(8,128)(2,1)}, ...), condition=%wide.region_9.10_spmd.clone.clone, body=%wide.region_6.9_spmd.clone.sunk.clone | while | flops 214302208 | bytes 10438257 | solution.py:123
  478.6 2.3 fusion.49
  480.9 2.3 collective-permute-start.8
  483.4 3.5 collective-permute-start.4
  487.0 2.1 collective-permute-start.5
  489.1 2.6 collective-permute-done.4
  491.7 5.6 fusion.119
  497.3 14.0 %collective-permute-done.5 = bf16[15,1536]{0,1:T(8,128)(2,1)S(1)} collective-permute-done((bf16[15,1536]{0,1:T(8,128)(2,1)S(1)}, bf16[15,1536]{0,1:T(8,128)(2,1)S(1)}, u32[]{:S(2)}, u32[]{:S(2)}) %collective-permute-start.5) | collective-permute-done | bytes 46112 | tf_op jit(solution)/shard_map/ppermute | solution.py:28
  511.3 6.0 fusion.135
  520.8 3.7 fusion.118
  524.7 4.4 fusion.134
  529.3 2.8 stack.143
  532.1 8.9 %collective-permute-done.9 = bf16[2,256,1536]{1,2,0:T(8,128)(2,1)} collective-permute-done((bf16[2,256,1536]{1,2,0:T(8,128)(2,1)}, bf16[2,256,1536]{1,2,0:T(8,128)(2,1)}, u32[]{:S(2)}, u32[]{:S(2)}) %collective-permute-start.9) | collective-permute-done | bytes 1572896 | tf_op jit(solution)/shard_map/ppermute | solution.py:17
  541.0 4.0 fusion.55
  548.3 27.4 %collective-permute-done.10 = bf16[2,256,1536]{1,2,0:T(8,128)(2,1)} collective-permute-done((bf16[2,256,1536]{1,2,0:T(8,128)(2,1)}, bf16[2,256,1536]{1,2,0:T(8,128)(2,1)}, u32[]{:S(2)}, u32[]{:S(2)}) %collective-permute-start.10) | collective-permute-done | bytes 1572896 | tf_op jit(solution)/shard_map/ppermute | solution.py:17
  575.7 4.0 fusion.47
  581.9 19.3 %fusion.88 = bf16[256,1536]{0,1:T(8,128)(2,1)S(1)} fusion(bf16[256,1536]{0,1:T(8,128)(2,1)S(1)} %bitcast.170, f32[1536]{0:T(1024)S(1)} %copy-done.36, f32[1536]{0:T(1024)S(1)} %copy-done.37, f32[1536]{0:T(1024)S(1)} %copy-done.8, f32[1536]{0:T(1024)S(1)} %copy-done.9, f32[1536]{0:T(1024)S(1)} %copy-done.10, f32[1536]{0:T(1024)S(1)} %copy-done.11, ...), kind=kLoop, calls=%fused_computation.280 | loop fusion | flops 71958528 | bytes 1855488 | tf_op jit(solution)/shard_map/convert_element_type | solution.py:101
  602.4 2.8 reduce_sum.347
  605.1 2.7 fusion.57
  (479 shorter events, 318.2 us)
Async XLA Ops:
  7.2 595.2 %all-gather.4.cloned.1.call-start = ((), (), s32[]{:S(2)}) async-start(), calls=%async_computation | async-start | bytes 3342336 | tf_op jit(solution)/shard_map/all_gather | solution.py:103
  9.0 49.9 %copy-start.5 = (bf16[256,1536]{1,0:T(8,128)(2,1)S(1)}, bf16[256,1536]{1,0:T(8,128)(2,1)}, u32[]{:S(2)}) copy-start(bf16[256,1536]{1,0:T(8,128)(2,1)} %param.15) | copy-start | bytes 2359300
  9.0 56.5 %copy-start.38 = (s32[2,4]{1,0:T(2,128)S(1)}, s32[2,4]{1,0:T(2,128)}, u32[]{:S(2)}) copy-start(s32[2,4]{1,0:T(2,128)} %param.13) | copy-start | bytes 100
  10.4 21.0 %collective-permute-start = (bf16[2,256,1536]{1,2,0:T(8,128)(2,1)S(1)}, bf16[2,256,1536]{1,2,0:T(8,128)(2,1)S(1)}, u32[]{:S(2)}, u32[]{:S(2)}) collective-permute-start(bf16[2,256,1536]{1,2,0:T(8,128)(2,1)S(1)} %get-tuple-element.321), channel_id=1, source_target_pairs={{0,1},{1,2},{2,3},{3,4},{4,5},{5,6},{6,7},{7,8},{8,9},{9,10},{10,1... | collective-permute-start | bytes 4718600 | tf_op jit(solution)/shard_map/ppermute | solution.py:17
  32.6 21.7 %collective-permute-start.1 = (bf16[2,256,1536]{1,2,0:T(8,128)(2,1)S(1)}, bf16[2,256,1536]{1,2,0:T(8,128)(2,1)}, u32[]{:S(2)}, u32[]{:S(2)}) collective-permute-start(bf16[2,256,1536]{1,2,0:T(8,128)(2,1)S(1)} %collective-permute-done), channel_id=1, source_target_pairs={{0,1},{1,2},{2,3},{3,4},{4,5},{5,6},{6,7},{7,8},{8,9},{9,10},{10,1... | collective-permute-start | bytes 4718600 | tf_op jit(solution)/shard_map/ppermute | solution.py:17
  54.4 22.1 %collective-permute-start.2 = (bf16[2,256,1536]{1,2,0:T(8,128)(2,1)}, bf16[2,256,1536]{1,2,0:T(8,128)(2,1)}, u32[]{:S(2)}, u32[]{:S(2)}) collective-permute-start(bf16[2,256,1536]{1,2,0:T(8,128)(2,1)} %collective-permute-done.1), channel_id=1, source_target_pairs={{0,1},{1,2},{2,3},{3,4},{4,5},{5,6},{6,7},{7,8},{8,9},{9,10},{10,1... | collective-permute-start | bytes 4718600 | tf_op jit(solution)/shard_map/ppermute | solution.py:17
  59.8 21.0 %collective-permute-start.7 = (bf16[15,1536]{0,1:T(8,128)(2,1)}, bf16[15,1536]{0,1:T(8,128)(2,1)S(1)}, u32[]{:S(2)}, u32[]{:S(2)}) collective-permute-start(bf16[15,1536]{0,1:T(8,128)(2,1)} %copy.94), channel_id=1, source_target_pairs={{0,1},{1,2},{2,3},{3,4},{4,5},{5,6},{6,7},{7,8},{8,9},{9,10},{10,1... | collective-permute-start | bytes 138248 | tf_op jit(solution)/shard_map/ppermute | solution.py:25
  62.7 42.4 %collective-permute-start.6 = (bf16[15,1536]{0,1:T(8,128)(2,1)}, bf16[15,1536]{0,1:T(8,128)(2,1)}, u32[]{:S(2)}, u32[]{:S(2)}) collective-permute-start(bf16[15,1536]{0,1:T(8,128)(2,1)} %copy.91), channel_id=1, source_target_pairs={{1,0},{2,1},{3,2},{4,3},{5,4},{6,5},{7,6},{8,7},{9,8},{10,9},{11,1... | collective-permute-start | bytes 138248 | tf_op jit(solution)/shard_map/ppermute | solution.py:28
  72.8 59.7 %copy-start.4 = (bf16[2,256,1536]{1,2,0:T(8,128)(2,1)S(1)}, bf16[2,256,1536]{1,2,0:T(8,128)(2,1)}, u32[]{:S(2)}) copy-start(bf16[2,256,1536]{1,2,0:T(8,128)(2,1)} %copy-done.3) | copy-start | bytes 4718596
  76.5 62.9 %collective-permute-start.3 = (bf16[2,256,1536]{1,2,0:T(8,128)(2,1)}, bf16[2,256,1536]{1,2,0:T(8,128)(2,1)S(1)}, u32[]{:S(2)}, u32[]{:S(2)}) collective-permute-start(bf16[2,256,1536]{1,2,0:T(8,128)(2,1)} %collective-permute-done.2), channel_id=1, source_target_pairs={{0,1},{1,2},{2,3},{3,4},{4,5},{5,6},{6,7},{7,8},{8,9},{9,10},{10,1... | collective-permute-start | bytes 4718600 | tf_op jit(solution)/shard_map/ppermute | solution.py:17
  478.6 38.7 %copy-start = (f32[24,1280,64]{1,2,0:T(8,128)S(1)}, f32[24,1280,64]{1,2,0:T(8,128)}, u32[]{:S(2)}) copy-start(f32[24,1280,64]{1,2,0:T(8,128)} %get-tuple-element.94) | copy-start | bytes 23592964
  478.6 38.7 %copy-start.1 = (f32[24,1280,64]{1,2,0:T(8,128)S(1)}, f32[24,1280,64]{1,2,0:T(8,128)}, u32[]{:S(2)}) copy-start(f32[24,1280,64]{1,2,0:T(8,128)} %get-tuple-element.93) | copy-start | bytes 23592964
  480.9 36.4 %collective-permute-start.8 = (bf16[2,256,1536]{1,2,0:T(8,128)(2,1)S(1)}, bf16[2,256,1536]{1,2,0:T(8,128)(2,1)S(1)}, u32[]{:S(2)}, u32[]{:S(2)}) collective-permute-start(bf16[2,256,1536]{1,2,0:T(8,128)(2,1)S(1)} %fusion.49), channel_id=1, source_target_pairs={{1,0},{2,1},{3,2},{4,3},{5,4},{6,5},{7,6},{8,7},{9,8},{10,9},{11,1... | collective-permute-start | bytes 4718600 | tf_op jit(solution)/shard_map/ppermute | solution.py:17
  483.4 8.2 %collective-permute-start.4 = (bf16[15,1536]{0,1:T(8,128)(2,1)S(1)}, bf16[15,1536]{0,1:T(8,128)(2,1)S(1)}, u32[]{:S(2)}, u32[]{:S(2)}) collective-permute-start(bf16[15,1536]{0,1:T(8,128)(2,1)S(1)} %bitcast.184), channel_id=1, source_target_pairs={{0,1},{1,2},{2,3},{3,4},{4,5},{5,6},{6,7},{7,8},{8,9},{9,10},{10,1... | collective-permute-start | bytes 138248 | tf_op jit(solution)/shard_map/ppermute | solution.py:25
  487.0 24.3 %collective-permute-start.5 = (bf16[15,1536]{0,1:T(8,128)(2,1)S(1)}, bf16[15,1536]{0,1:T(8,128)(2,1)S(1)}, u32[]{:S(2)}, u32[]{:S(2)}) collective-permute-start(bf16[15,1536]{0,1:T(8,128)(2,1)S(1)} %bitcast.183), channel_id=1, source_target_pairs={{1,0},{2,1},{3,2},{4,3},{5,4},{6,5},{7,6},{8,7},{9,8},{10,9},{11,1... | collective-permute-start | bytes 138248 | tf_op jit(solution)/shard_map/ppermute | solution.py:28
  518.9 22.0 %collective-permute-start.9 = (bf16[2,256,1536]{1,2,0:T(8,128)(2,1)}, bf16[2,256,1536]{1,2,0:T(8,128)(2,1)}, u32[]{:S(2)}, u32[]{:S(2)}) collective-permute-start(bf16[2,256,1536]{1,2,0:T(8,128)(2,1)} %fusion.52), channel_id=1, source_target_pairs={{1,0},{2,1},{3,2},{4,3},{5,4},{6,5},{7,6},{8,7},{9,8},{10,9},{11,1... | collective-permute-start | bytes 4718600 | tf_op jit(solution)/shard_map/ppermute | solution.py:17
  545.0 30.8 %collective-permute-start.10 = (bf16[2,256,1536]{1,2,0:T(8,128)(2,1)}, bf16[2,256,1536]{1,2,0:T(8,128)(2,1)}, u32[]{:S(2)}, u32[]{:S(2)}) collective-permute-start(bf16[2,256,1536]{1,2,0:T(8,128)(2,1)} %fusion.55), channel_id=1, source_target_pairs={{1,0},{2,1},{3,2},{4,3},{5,4},{6,5},{7,6},{8,7},{9,8},{10,9},{11,1... | collective-permute-start | bytes 4718600 | tf_op jit(solution)/shard_map/ppermute | solution.py:17
  548.1 33.6 %copy-start.8 = (f32[1536]{0:T(1024)S(1)}, f32[1536]{0:T(1024)}, u32[]{:S(2)}) copy-start(f32[1536]{0:T(1024)} %get-tuple-element.249) | copy-start | bytes 18436
  548.1 33.6 %copy-start.9 = (f32[1536]{0:T(1024)S(1)}, f32[1536]{0:T(1024)}, u32[]{:S(2)}) copy-start(f32[1536]{0:T(1024)} %get-tuple-element.250) | copy-start | bytes 18436
  548.1 33.6 %copy-start.10 = (f32[1536]{0:T(1024)S(1)}, f32[1536]{0:T(1024)}, u32[]{:S(2)}) copy-start(f32[1536]{0:T(1024)} %get-tuple-element.251) | copy-start | bytes 18436
  548.1 33.6 %copy-start.11 = (f32[1536]{0:T(1024)S(1)}, f32[1536]{0:T(1024)}, u32[]{:S(2)}) copy-start(f32[1536]{0:T(1024)} %get-tuple-element.252) | copy-start | bytes 18436
  548.1 33.6 %copy-start.12 = (f32[1536]{0:T(1024)S(1)}, f32[1536]{0:T(1024)}, u32[]{:S(2)}) copy-start(f32[1536]{0:T(1024)} %get-tuple-element.253) | copy-start | bytes 18436
  548.1 33.6 %copy-start.13 = (f32[1536]{0:T(1024)S(1)}, f32[1536]{0:T(1024)}, u32[]{:S(2)}) copy-start(f32[1536]{0:T(1024)} %get-tuple-element.254) | copy-start | bytes 18436
  548.1 33.6 %copy-start.14 = (f32[1536]{0:T(1024)S(1)}, f32[1536]{0:T(1024)}, u32[]{:S(2)}) copy-start(f32[1536]{0:T(1024)} %get-tuple-element.255) | copy-start | bytes 18436
  548.1 33.6 %copy-start.15 = (f32[1536]{0:T(1024)S(1)}, f32[1536]{0:T(1024)}, u32[]{:S(2)}) copy-start(f32[1536]{0:T(1024)} %get-tuple-element.256) | copy-start | bytes 18436
  548.1 33.6 %copy-start.16 = (f32[1536]{0:T(1024)S(1)}, f32[1536]{0:T(1024)}, u32[]{:S(2)}) copy-start(f32[1536]{0:T(1024)} %get-tuple-element.257) | copy-start | bytes 18436
  548.1 33.6 %copy-start.17 = (f32[1536]{0:T(1024)S(1)}, f32[1536]{0:T(1024)}, u32[]{:S(2)}) copy-start(f32[1536]{0:T(1024)} %get-tuple-element.258) | copy-start | bytes 18436
  548.1 33.6 %copy-start.18 = (f32[1536]{0:T(1024)S(1)}, f32[1536]{0:T(1024)}, u32[]{:S(2)}) copy-start(f32[1536]{0:T(1024)} %get-tuple-element.259) | copy-start | bytes 18436
  548.1 33.6 %copy-start.19 = (f32[1536]{0:T(1024)S(1)}, f32[1536]{0:T(1024)}, u32[]{:S(2)}) copy-start(f32[1536]{0:T(1024)} %get-tuple-element.260) | copy-start | bytes 18436
  548.2 33.6 %copy-start.20 = (f32[1536]{0:T(1024)S(1)}, f32[1536]{0:T(1024)}, u32[]{:S(2)}) copy-start(f32[1536]{0:T(1024)} %get-tuple-element.261) | copy-start | bytes 18436
  548.2 33.6 %copy-start.21 = (f32[1536]{0:T(1024)S(1)}, f32[1536]{0:T(1024)}, u32[]{:S(2)}) copy-start(f32[1536]{0:T(1024)} %get-tuple-element.262) | copy-start | bytes 18436
  548.2 33.6 %copy-start.22 = (f32[1536]{0:T(1024)S(1)}, f32[1536]{0:T(1024)}, u32[]{:S(2)}) copy-start(f32[1536]{0:T(1024)} %get-tuple-element.263) | copy-start | bytes 18436
  548.2 33.6 %copy-start.23 = (f32[1536]{0:T(1024)S(1)}, f32[1536]{0:T(1024)}, u32[]{:S(2)}) copy-start(f32[1536]{0:T(1024)} %get-tuple-element.264) | copy-start | bytes 18436
  548.2 33.6 %copy-start.24 = (f32[1536]{0:T(1024)S(1)}, f32[1536]{0:T(1024)}, u32[]{:S(2)}) copy-start(f32[1536]{0:T(1024)} %get-tuple-element.265) | copy-start | bytes 18436
  548.2 33.6 %copy-start.25 = (f32[1536]{0:T(1024)S(1)}, f32[1536]{0:T(1024)}, u32[]{:S(2)}) copy-start(f32[1536]{0:T(1024)} %get-tuple-element.266) | copy-start | bytes 18436
  548.2 33.6 %copy-start.26 = (f32[1536]{0:T(1024)S(1)}, f32[1536]{0:T(1024)}, u32[]{:S(2)}) copy-start(f32[1536]{0:T(1024)} %get-tuple-element.267) | copy-start | bytes 18436
  548.2 33.6 %copy-start.27 = (f32[1536]{0:T(1024)S(1)}, f32[1536]{0:T(1024)}, u32[]{:S(2)}) copy-start(f32[1536]{0:T(1024)} %get-tuple-element.268) | copy-start | bytes 18436
  548.2 33.6 %copy-start.28 = (f32[1536]{0:T(1024)S(1)}, f32[1536]{0:T(1024)}, u32[]{:S(2)}) copy-start(f32[1536]{0:T(1024)} %get-tuple-element.269) | copy-start | bytes 18436
  548.3 33.6 %copy-start.29 = (f32[1536]{0:T(1024)S(1)}, f32[1536]{0:T(1024)}, u32[]{:S(2)}) copy-start(f32[1536]{0:T(1024)} %get-tuple-element.270) | copy-start | bytes 18436
  548.3 33.6 %copy-start.30 = (f32[1536]{0:T(1024)S(1)}, f32[1536]{0:T(1024)}, u32[]{:S(2)}) copy-start(f32[1536]{0:T(1024)} %get-tuple-element.271) | copy-start | bytes 18436
  548.3 33.6 %copy-start.31 = (f32[1536]{0:T(1024)S(1)}, f32[1536]{0:T(1024)}, u32[]{:S(2)}) copy-start(f32[1536]{0:T(1024)} %get-tuple-element.272) | copy-start | bytes 18436
  548.3 33.6 %copy-start.32 = (f32[1536]{0:T(1024)S(1)}, f32[1536]{0:T(1024)}, u32[]{:S(2)}) copy-start(f32[1536]{0:T(1024)} %get-tuple-element.273) | copy-start | bytes 18436
  548.3 33.6 %copy-start.33 = (f32[1536]{0:T(1024)S(1)}, f32[1536]{0:T(1024)}, u32[]{:S(2)}) copy-start(f32[1536]{0:T(1024)} %get-tuple-element.274) | copy-start | bytes 18436
  548.3 33.6 %copy-start.34 = (f32[1536]{0:T(1024)S(1)}, f32[1536]{0:T(1024)}, u32[]{:S(2)}) copy-start(f32[1536]{0:T(1024)} %get-tuple-element.275) | copy-start | bytes 18436
  548.3 33.6 %copy-start.35 = (f32[1536]{0:T(1024)S(1)}, f32[1536]{0:T(1024)}, u32[]{:S(2)}) copy-start(f32[1536]{0:T(1024)} %get-tuple-element.276) | copy-start | bytes 18436
  548.3 33.6 %copy-start.36 = (f32[1536]{0:T(1024)S(1)}, f32[1536]{0:T(1024)}, u32[]{:S(2)}) copy-start(f32[1536]{0:T(1024)} %get-tuple-element.277) | copy-start | bytes 18436
  548.3 33.6 %copy-start.37 = (f32[1536]{0:T(1024)S(1)}, f32[1536]{0:T(1024)}, u32[]{:S(2)}) copy-start(f32[1536]{0:T(1024)} %get-tuple-element.278) | copy-start | bytes 18436
  579.7 25.4 %collective-permute-start.11 = (bf16[2,256,1536]{1,2,0:T(8,128)(2,1)}, bf16[2,256,1536]{1,2,0:T(8,128)(2,1)}, u32[]{:S(2)}, u32[]{:S(2)}) collective-permute-start(bf16[2,256,1536]{1,2,0:T(8,128)(2,1)} %fusion.47), channel_id=1, source_target_pairs={{1,0},{2,1},{3,2},{4,3},{5,4},{6,5},{7,6},{8,7},{9,8},{10,9},{11,1... | collective-permute-start | bytes 4718600 | tf_op jit(solution)/shard_map/ppermute | solution.py:17
  (4 other events, 27.4 us)
Sparse Core Ops, SparseCore 0:
  532.2 49.1 all-gather.3
